TPU v7x, 256 devices: a whole 4x4x8 slice. The times are simulated.
256 devices in a mesh: ctx: 8 (over z), expert: 32 (over y, x, core).
Axes of the slice: x: 4, y: 4, z: 8, core: 2. Of those that a mesh axis runs over, the one named last changes fastest.
Arguments:
- tokens: bfloat16 [32, 1024, 1024], P('expert', 'ctx'), may hold values from -6 to 6
- chain_ids: int32 [32, 1024], P('expert', 'ctx'), may hold values from 0 to 7, never falling along the last dimension, each value on 1 to 256 neighbouring positions
- route_ids: int32 [32, 1024, 6], P('expert', 'ctx'), may hold values from 0 to 31, all different within a row; in each aligned block of 128 rows (0 to 127, 128 to 255, ..., all dimensions but the last counted through in order) at most 32 rows name the same one
- route_weights: float32 [32, 1024, 6], P('expert', 'ctx'), may hold values from 0.1 to 0.5
- attn_gain: float32 [1024], replicated, may hold values from 0.6 to 12
- ffn_gain: float32 [1024], replicated, may hold values from 0.1 to 1.9
- chain_bias: float32 [8], replicated, may hold values from 0.5 to 2.5
- w_qkv: bfloat16 [3, 1024, 1024], P(None, 'expert', 'ctx'), may hold values from -0.1875 to 0.1875
- w_out: bfloat16 [1024, 1024], P('ctx', 'expert'), may hold values from -0.75 to 0.75
- w_gateup: bfloat16 [32, 1024, 2816], P('expert'), may hold values from -0.1875 to 0.1875
- w_down: bfloat16 [32, 1408, 1024], P('expert'), may hold values from -0.15625 to 0.15625
Outputs:
- layer_out: bfloat16 [32, 1024, 1024], P('expert', 'ctx')
Inputs may be any that keep to these rules, and one draw needn't show every extreme that they name: `route_ids`: each residue names 6 different experts. Among the 128 residues of one device (aligned blocks of the residues in order, crop after crop), no expert is named by more than 32 of them, and in every draw some expert is named by exactly 32. `chain_ids`: chain numbers never fall along a crop; a chain spans 1 to 256 residues, and some chain exactly that many.
All inputs are finite; a program needn't handle non-finite values.
Results may differ from a plain program's by a relative error of at most 0.02.
The roundings to bfloat16 on the way count: a program that leaves them out, or rounds other values in their place, can miss the bound.
Values may be sent and summed in bfloat16 or wider, within the bound.
No kernel may reach another device: no remote copies, remote signals or barrier semaphores. Data moves between devices by JAX's collectives and lax.ppermute only.
A program may use at most 64 MiB of HBM per device.

v0:
```python
import math
import jax
import jax.numpy as jnp
from jax import lax
from jax.sharding import PartitionSpec as P


def rms_scale(values, gain):
    wide = values.astype(jnp.float32)
    return wide * lax.rsqrt(jnp.mean(wide * wide, axis=-1, keepdims=True) + 1e-05) * gain


def attend(query, key, value, chains, bias):
    length = query.shape[0]
    group = bias.shape[0]
    head_dim = query.shape[1] // group
    block = min(512, length)
    scale = 1.0 / math.sqrt(head_dim)
    keys = key.reshape(length, group, head_dim)
    values = value.reshape(length, group, head_dim)
    query_blocks = query.reshape(length // block, block, group, head_dim)
    chain_blocks = chains.reshape(length // block, block)

    def one_block(items):
        q_block, c_block = items
        scores = (
            jnp.einsum("qhd,khd->hqk", q_block, keys, preferred_element_type=jnp.float32) * scale
        )
        same = (c_block[:, None] == chains[None, :]).astype(jnp.float32)
        scores = scores + bias[:, None, None] * same[None]
        top = jnp.max(scores, axis=-1, keepdims=True)
        raised = jnp.exp(scores - top)
        probs = (raised / jnp.sum(raised, axis=-1, keepdims=True)).astype(jnp.bfloat16)
        return jnp.einsum("hqk,khd->qhd", probs, values, preferred_element_type=jnp.float32).astype(
            jnp.bfloat16
        )

    return lax.map(one_block, (query_blocks, chain_blocks)).reshape(length, group * head_dim)


def per_device(
    tokens,
    chain_ids,
    route_ids,
    route_weights,
    attn_gain,
    ffn_gain,
    chain_bias,
    w_qkv,
    w_out,
    w_gateup,
    w_down,
):
    tok = tokens.shape[1]
    width = tokens.shape[2]
    inputs = tokens[0]
    normed = rms_scale(inputs, attn_gain).astype(jnp.bfloat16)
    chains = lax.all_gather(chain_ids[0], "ctx", axis=0, tiled=True)
    groups = lax.axis_size("ctx")
    per_group = chain_bias.shape[0] // groups
    bias = lax.dynamic_slice_in_dim(chain_bias, lax.axis_index("ctx") * per_group, per_group)
    qkv_columns, out_full_rows = (
        lax.all_gather(w_qkv, "ctx", axis=2, tiled=True),
        lax.all_gather(w_out, "ctx", axis=0, tiled=True),
    )
    projected = jnp.einsum(
        "tr,ird->itd",
        normed,
        lax.all_gather(qkv_columns, "expert", axis=1, tiled=True),
        preferred_element_type=jnp.float32,
    ).astype(jnp.bfloat16)
    regrouped = lax.all_to_all(projected, "ctx", split_axis=2, concat_axis=1, tiled=True)
    attended = attend(regrouped[0], regrouped[1], regrouped[2], chains, bias)
    local_rows = lax.all_to_all(attended, "ctx", split_axis=0, concat_axis=1, tiled=True)
    mixed = inputs.astype(jnp.float32) + jnp.dot(
        local_rows,
        lax.all_gather(out_full_rows, "expert", axis=1, tiled=True),
        preferred_element_type=jnp.float32,
    )
    ffn_in = rms_scale(mixed, ffn_gain).astype(jnp.bfloat16)
    held = w_gateup.shape[0]
    experts = lax.axis_size("expert") * held
    topk = route_ids.shape[2]
    cap = min(tok, tok * topk * 4 // (experts * 3))
    hidden = w_down.shape[1]
    flat_ids = route_ids[0].reshape(-1)
    onehot = (flat_ids[:, None] == jnp.arange(experts, dtype=jnp.int32)[None, :]).astype(jnp.int32)
    rank = jnp.sum((jnp.cumsum(onehot, axis=0) - onehot) * onehot, axis=1)
    slots = flat_ids * cap + rank
    select = jnp.sum(
        (
            slots.reshape(tok, topk)[:, :, None]
            == jnp.arange(experts * cap, dtype=jnp.int32)[None, None, :]
        ).astype(jnp.bfloat16),
        axis=1,
    )
    outgoing = lax.dot_general(
        select, ffn_in, (((0,), (0,)), ((), ())), preferred_element_type=jnp.float32
    )
    outgoing = outgoing.astype(jnp.bfloat16).reshape(experts, cap, width)
    block = lax.all_to_all(outgoing, "expert", split_axis=0, concat_axis=0, tiled=True)
    count = block.shape[1]
    grouped = block.reshape(-1, held, count, width)
    both = jnp.einsum("sxcd,xdf->sxcf", grouped, w_gateup, preferred_element_type=jnp.float32)
    active = (jax.nn.silu(both[..., :hidden]) * both[..., hidden:]).astype(jnp.bfloat16)
    result = jnp.einsum(
        "sxcf,xfd->sxcd", active, w_down, preferred_element_type=jnp.float32
    ).astype(jnp.bfloat16)
    returned = lax.all_to_all(
        result.reshape(-1, count, width), "expert", split_axis=0, concat_axis=0, tiled=True
    )
    picked = jnp.take(returned.reshape(-1, width), slots, axis=0).reshape(tok, topk, width)
    weights = route_weights[0]
    moe_sum = mixed
    for route in range(topk):
        moe_sum = moe_sum + weights[:, route : route + 1] * picked[:, route].astype(jnp.float32)
    return moe_sum.astype(jnp.bfloat16)[None]


def solution(mesh):
    placed = (
        P("expert", "ctx", None),
        P("expert", "ctx"),
        P("expert", "ctx", None),
        P("expert", "ctx", None),
        P(),
        P(),
        P(),
        P(None, "expert", "ctx"),
        P("ctx", "expert"),
        P("expert", None, None),
        P("expert", None, None),
    )
    return jax.shard_map(
        per_device, mesh=mesh, in_specs=placed, out_specs=P("expert", "ctx", None), check_vma=False
    )
```

profile of v0, /device:TPU:1, one launch (start us, length us, event | category | flops | bytes accessed | tf_op | source)
XLA Modules:
  0.0 299.5 jit_solution(6906347522959631811)
XLA Ops:
  6.5 23.7 %all_gather.15 = bf16[3,32,1024]{2,1,0:T(8,128)(2,1)} all-gather(bf16[3,32,128]{2,1,0:T(8,128)(2,1)} %param.20), channel_id=1, replica_groups=mesh['ctx'=8,'expert'=32] {'ctx'}, dimensions={2}, use_global_device_ids=true | all-gather | bytes 221184 | tf_op jit(solution)/shard_map/all_gather | solution.py:63
  30.3 1.1 fusion.22
  31.4 57.7 %all-gather.4.cloned.1.call-done = bf16[3,1024,1024]{2,1,0:T(8,128)(2,1)} async-done(((bf16[3,32,1024]{2,1,0:T(8,128)(2,1)}), bf16[3,1024,1024]{2,1,0:T(8,128)(2,1)}) %all-gather.4.cloned.1.call-update) | async-done | bytes 6291472 | tf_op jit(solution)/shard_map/all_gather | solution.py:69
  89.0 4.8 %fusion.21 = bf16[3,128,1024]{2,1,0:T(8,128)(2,1)} fusion(bf16[3,1024,1024]{2,1,0:T(8,128)(2,1)} %all-gather.4.cloned.1.call-done, bf16[1,128,1024]{2,1,0:T(8,128)(2,1)} %param.13, f32[1024]{0:T(1024)} %param.17, f32[128]{0:T(128)S(1)} %add_rsqrt_fusion.1), kind=kOutput, calls=%fused_computation.28 | convolution fusion | flops 806223872 | bytes 7344640 | tf_op jit(solution)/shard_map/tr,ird->itd/dot_general | solution.py:66
  93.9 2.4 copy.69
  96.3 6.7 %all-to-all-start = ((bf16[3,128,1024]{1,0,2:T(4,128)(2,1)}), bf16[3,128,1024]{1,0,2:T(4,128)(2,1)}, u32[]{:S(2)}, u32[]{:S(2)}) async-start(bf16[3,128,1024]{1,0,2:T(4,128)(2,1)} %copy.69), calls=%async_computation | async-start | bytes 2097152 | tf_op jit(solution)/shard_map/all_to_all | solution.py:72
  103.1 39.4 %all_gather.18 = bf16[1024,32]{0,1:T(8,128)(2,1)} all-gather(bf16[128,32]{0,1:T(8,128)(2,1)S(1)} %copy-done.6), channel_id=1, replica_groups=mesh['ctx'=8,'expert'=32] {'ctx'}, dimensions={0}, use_global_device_ids=true | all-gather | bytes 73728 | tf_op jit(solution)/shard_map/all_gather | solution.py:64
  143.0 11.5 %all-gather = s32[1,1024]{1,0:T(1,128)S(1)} all-gather(s32[1,128]{1,0:T(1,128)S(1)} %copy-done.9), channel_id=2, replica_groups=mesh['ctx'=8,'expert'=32] {'ctx'}, dimensions={1}, use_global_device_ids=true | all-gather | bytes 4608 | tf_op jit(solution)/shard_map/all_gather | solution.py:58
  155.7 1.7 reduce-window.6
  158.3 1.3 copy.70
  160.5 1.8 copy.71
  162.3 0.8 copy.72
  163.1 0.8 copy.73
  164.0 8.2 %while.10 = (s32[]{:T(128)}, bf16[2,512,1,128]{3,1,2,0:T(8,128)(2,1)}, bf16[2,512,1,128]{3,1,2,0:T(8,128)(2,1)}, bf16[1024,1,128]{2,0,1:T(8,128)(2,1)}, s32[2,51...) while((s32[]{:T(128)}, ...), condition=%wide.region_4.5_spmd, body=%wide.region_1.4_spmd.sunk | while | flops 273742848 | bytes 10245305 | solution.py:38
  164.0 2.3 fusion.58
  168.1 2.3 fusion.58
  172.2 4.2 %all-to-all-start.1 = ((bf16[8,128,128]{2,1,0:T(8,128)(2,1)}), bf16[8,128,128]{2,1,0:T(8,128)(2,1)S(1)}, u32[]{:S(2)}, u32[]{:S(2)}) async-start(bf16[8,128,128]{2,1,0:T(8,128)(2,1)} %bitcast.176), calls=%async_computation.1 | async-start | bytes 524288 | tf_op jit(solution)/shard_map/all_to_all | solution.py:74
  176.8 1.1 fusion.20
  177.9 7.9 %all-to-all-done.1 = bf16[8,128,128]{2,1,0:T(8,128)(2,1)S(1)} async-done(((bf16[8,128,128]{2,1,0:T(8,128)(2,1)}), bf16[8,128,128]{2,1,0:T(8,128)(2,1)S(1)}, u32[]{:S(2)}, u32[]{:S(2)}) %all-to-all-start.1) | async-done | bytes 262176 | tf_op jit(solution)/shard_map/all_to_all | solution.py:74
  185.8 0.9 copy.75
  186.6 6.5 %all-gather.6.cloned.1.call-done = bf16[1024,1024]{0,1:T(8,128)(2,1)} async-done(((bf16[1024,32]{0,1:T(8,128)(2,1)}), bf16[1024,1024]{0,1:T(8,128)(2,1)}) %all-gather.6.cloned.1.call-update) | async-done | bytes 2097168 | tf_op jit(solution)/shard_map/all_gather | solution.py:77
  193.2 2.6 multiply_reduce_fusion
  195.8 0.8 convolution_convert_fusion.1
  196.6 37.6 %all_to_all.44 = bf16[32,32,1024]{2,1,0:T(8,128)(2,1)S(1)} all-to-all(bf16[32,32,1024]{2,1,0:T(8,128)(2,1)S(1)} %bitcast.172), channel_id=1, replica_groups=mesh['ctx'=8,'expert'=32] {'expert'}, dimensions={0} | all-to-all | bytes 4194304 | tf_op jit(solution)/shard_map/all_to_all | solution.py:101
  234.2 6.1 %convolution_bitcast_fusion = f32[32,1,32,2816]{3,2,0,1:T(8,128)S(1)} fusion(bf16[32,32,1024]{2,1,0:T(8,128)(2,1)S(1)} %all_to_all.44, bf16[1,1024,2816]{2,1,0:T(8,128)(2,1)S(1)} %copy-done.10), kind=kOutput, calls=%fused_computation.14 | convolution fusion | flops 5905580032 | bytes 19398656 | tf_op jit(solution)/shard_map/sxcd,xdf->sxcf/dot_general | solution.py:104
  240.4 4.8 %fusion.15 = bf16[32,32,1024]{2,1,0:T(8,128)(2,1)} fusion(bf16[1,1408,1024]{2,1,0:T(8,128)(2,1)S(1)} %copy-done, f32[32,1,32,2816]{3,2,0,1:T(8,128)S(1)} %convolution_bitcast_fusion), kind=kOutput, calls=%fused_computation.23 | convolution fusion | flops 2962489344 | bytes 16515072 | tf_op jit(solution)/shard_map/sxcf,xfd->sxcd/dot_general | solution.py:106
  245.2 4.9 %all-to-all-start.3 = ((bf16[32,32,1024]{2,1,0:T(8,128)(2,1)}), bf16[32,32,1024]{2,1,0:T(8,128)(2,1)}, u32[]{:S(2)}, u32[]{:S(2)}) async-start(bf16[32,32,1024]{2,1,0:T(8,128)(2,1)} %fusion.15), calls=%async_computation.3 | async-start | bytes 4194304 | tf_op jit(solution)/shard_map/all_to_all | solution.py:109
  250.4 27.6 %all-to-all-done.3 = bf16[32,32,1024]{2,1,0:T(8,128)(2,1)} async-done(((bf16[32,32,1024]{2,1,0:T(8,128)(2,1)}), bf16[32,32,1024]{2,1,0:T(8,128)(2,1)}, u32[]{:S(2)}, u32[]{:S(2)}) %all-to-all-start.3) | async-done | bytes 2097184 | tf_op jit(solution)/shard_map/all_to_all | solution.py:109
  278.0 6.4 %gather_fusion = bf16[768,1024]{1,0:T(8,128)(2,1)} fusion(bf16[1024,1024]{1,0:T(8,128)(2,1)} %bitcast.38, s32[1024]{0:T(1024)S(1)} %pad_clamp_fusion), kind=kCustom, calls=%fused_computation | custom fusion | bytes 3148800 | tf_op jit(solution)/shard_map/jit(_take)/gather | solution.py:112
  284.4 3.7 %gather.7 = bf16[128,6,1024]{2,1,0:T(8,128)(2,1)} reshape(bf16[768,1024]{1,0:T(8,128)(2,1)} %gather_fusion) | data formatting | bytes 3145728 | tf_op jit(solution)/shard_map/jit(_take)/gather | solution.py:112
  288.1 3.4 %copy_select_fusion = bf16[128,6,1024]{2,0,1:T(8,128)(2,1)S(1)} fusion(bf16[128,6,1024]{2,1,0:T(8,128)(2,1)} %gather.7, pred[128,6]{0,1:T(8,128)(4,1)S(1)} %get-tuple-element.112), kind=kLoop, calls=%fused_computation.26 | loop fusion | flops 786432 | bytes 3146496 | tf_op jit(solution)/shard_map/jit(_take)/select_n | solution.py:112
  291.6 1.1 fusion.39
  (66 shorter events, 7.6 us)
Async XLA Ops:
  6.5 233.8 %copy-start = (bf16[1,1408,1024]{2,1,0:T(8,128)(2,1)S(1)}, bf16[1,1408,1024]{2,1,0:T(8,128)(2,1)}, u32[]{:S(2)}) copy-start(bf16[1,1408,1024]{2,1,0:T(8,128)(2,1)} %param.23) | copy-start | bytes 8650756
  6.5 82.5 %all-gather.4.cloned.1.call-start = ((), (), s32[]{:S(2)}) async-start(), calls=%async_computation.4 | async-start | bytes 6488064 | tf_op jit(solution)/shard_map/all_gather | solution.py:69
  93.9 9.2 %copy-start.6 = (bf16[128,32]{0,1:T(8,128)(2,1)S(1)}, bf16[128,32]{0,1:T(8,128)(2,1)}, u32[]{:S(2)}) copy-start(bf16[128,32]{0,1:T(8,128)(2,1)} %param.21) | copy-start | bytes 24580
  93.9 48.7 %copy-start.5 = (s32[1,128,6]{1,0,2:T(1,128)S(1)}, s32[1,128,6]{1,0,2:T(1,128)}, u32[]{:S(2)}) copy-start(s32[1,128,6]{1,0,2:T(1,128)} %param.15) | copy-start | bytes 9220
  93.9 49.1 %copy-start.9 = (s32[1,128]{1,0:T(1,128)S(1)}, s32[1,128]{1,0:T(1,128)}, u32[]{:S(2)}) copy-start(s32[1,128]{1,0:T(1,128)} %param.14) | copy-start | bytes 1540
  93.9 63.8 %copy-start.11 = (f32[8]{0:T(128)S(1)}, f32[8]{0:T(128)}, u32[]{:S(2)}) copy-start(f32[8]{0:T(128)} %param.19) | copy-start | bytes 100
  96.3 62.0 %all-to-all-start = ((bf16[3,128,1024]{1,0,2:T(4,128)(2,1)}), bf16[3,128,1024]{1,0,2:T(4,128)(2,1)}, u32[]{:S(2)}, u32[]{:S(2)}) async-start(bf16[3,128,1024]{1,0,2:T(4,128)(2,1)} %copy.69), calls=%async_computation | async-start | bytes 2097152 | tf_op jit(solution)/shard_map/all_to_all | solution.py:72
  103.0 90.1 %all-gather.6.cloned.1.call-start = ((), (), s32[]{:S(2)}) async-start(), calls=%async_computation.5 | async-start | bytes 2162688 | tf_op jit(solution)/shard_map/all_gather | solution.py:77
  164.0 2.8 copy-start.2
  164.0 2.8 copy-start.4
  167.4 0.7 copy-start.3
  168.1 2.8 copy-start.2
  168.1 2.8 copy-start.4
  171.5 0.7 copy-start.3
  172.2 13.6 %all-to-all-start.1 = ((bf16[8,128,128]{2,1,0:T(8,128)(2,1)}), bf16[8,128,128]{2,1,0:T(8,128)(2,1)S(1)}, u32[]{:S(2)}, u32[]{:S(2)}) async-start(bf16[8,128,128]{2,1,0:T(8,128)(2,1)} %bitcast.176), calls=%async_computation.1 | async-start | bytes 524288 | tf_op jit(solution)/shard_map/all_to_all | solution.py:74
  176.4 19.4 %copy-start.7 = (f32[1024]{0:T(1024)S(1)}, f32[1024]{0:T(1024)}, u32[]{:S(2)}) copy-start(f32[1024]{0:T(1024)} %param.18) | copy-start | bytes 12292
  193.2 2.6 copy-start.1
  195.8 38.4 %copy-start.10 = (bf16[1,1024,2816]{2,1,0:T(8,128)(2,1)S(1)}, bf16[1,1024,2816]{2,1,0:T(8,128)(2,1)}, u32[]{:S(2)}) copy-start(bf16[1,1024,2816]{2,1,0:T(8,128)(2,1)} %param.22) | copy-start | bytes 17301508
  245.2 5.2 %copy-start.8 = (f32[1,128,6]{1,0,2:T(1,128)S(1)}, f32[1,128,6]{1,0,2:T(1,128)}, u32[]{:S(2)}) copy-start(f32[1,128,6]{1,0,2:T(1,128)} %param.16) | copy-start | bytes 9220
  245.2 32.9 %all-to-all-start.3 = ((bf16[32,32,1024]{2,1,0:T(8,128)(2,1)}), bf16[32,32,1024]{2,1,0:T(8,128)(2,1)}, u32[]{:S(2)}, u32[]{:S(2)}) async-start(bf16[32,32,1024]{2,1,0:T(8,128)(2,1)} %fusion.15), calls=%async_computation.3 | async-start | bytes 4194304 | tf_op jit(solution)/shard_map/all_to_all | solution.py:109
Sparse Core Ops, SparseCore 0:
  30.4 58.5 all-gather.3
  142.7 50.4 all-gather.5
where the time goes:
time: 300 us
  blocking collectives  112 us (37%)
  waiting for transfers between devices  99.7 us (33%)
  matrix products  24.9 us (8%)
  local copies, waits for them, and re-layouts  22.7 us (8%)
  starting transfers between devices  15.9 us (5%)
  between operations  13.6 us (5%)
  other arithmetic  10.4 us (3%)
    all_gather x1, waiting for transfers between devices, per_device(): lax.all_gather(qkv_columns, 'expert', axis=1, tiled=True)  57.7 us
    all_gather x1, blocking collectives, per_device(): lax.all_gather(w_out, 'ctx', axis=0, tiled=True)  39.4 us
    all_to_all x1, blocking collectives, per_device(): lax.all_to_all(outgoing, 'expert', split_axis=0, concat_axis=0, tiled=True)  37.6 us
    all_to_all x1, waiting for transfers between devices, per_device(): lax.all_to_all(result.reshape(-1, count, width), 'expert', split_axis=0,...  27.6 us
    all_gather x1, blocking collectives, per_device(): lax.all_gather(w_qkv, 'ctx', axis=2, tiled=True)  23.7 us
    all_gather x1, blocking collectives, per_device(): chains = lax.all_gather(chain_ids[0], 'ctx', axis=0, tiled=True)  11.5 us
    gather x2, local copies, waits for them, and re-layouts, per_device(): jnp.take(returned.reshape(-1, width), slots, axis=0)  10.1 us
    all_to_all x1, waiting for transfers between devices, per_device(): lax.all_to_all(attended, 'ctx', split_axis=0, concat_axis=1, tiled=True)  7.86 us
  transfers between devices with their start and end apart: 5, of which 4 were waited for; matrix products, arithmetic and copies ran while one was open for 7% of the time, Pallas kernels for 0%

commit v1 on v0

--- a/solution.py
+++ b/solution.py
@@ -1,8 +1,27 @@
+import functools
 import math
 import jax
 import jax.numpy as jnp
 from jax import lax
 from jax.sharding import PartitionSpec as P
+
+
+def _map_unit(x_part, d0, bus_axis):
+    parts_n = lax.psum(1, axis_name=bus_axis)
+    mid_arr = [(p - 1, p) for p in range(1, parts_n)] + [(parts_n - 1, 0)]
+    right_arr = x_part
+    vals = [right_arr]
+    for _ in range(parts_n - 1):
+        right_arr = lax.ppermute(right_arr, axis_name=bus_axis, perm=mid_arr)
+        vals += [right_arr]
+    return jnp.roll(
+        jnp.concatenate([*reversed(vals)], axis=d0),
+        shift=(lax.axis_index(bus_axis) + 1) * right_arr.shape[d0],
+        axis=d0,
+    )
+
+
+scan_matrix = functools.partial(_map_unit, d0=0, bus_axis="ctx")
 
 
 def rms_scale(values, gain):
@@ -55,7 +74,7 @@
     width = tokens.shape[2]
     inputs = tokens[0]
     normed = rms_scale(inputs, attn_gain).astype(jnp.bfloat16)
-    chains = lax.all_gather(chain_ids[0], "ctx", axis=0, tiled=True)
+    chains = scan_matrix(chain_ids[0])
     groups = lax.axis_size("ctx")
     per_group = chain_bias.shape[0] // groups
     bias = lax.dynamic_slice_in_dim(chain_bias, lax.axis_index("ctx") * per_group, per_group)

time: 300 us -> 266 us (0.89)
  blocking collectives: 112 us -> 76 us
    all_gather x1, waiting for transfers between devices: 57.7 us -> 17.4 us  [per_device(): lax.all_gather(qkv_columns, 'expert', axis=1, tiled=True)]
    all_to_all x1, waiting for transfers between devices: 0.01 us -> 29.1 us  [per_device(): lax.all_to_all(projected, 'ctx', split_axis=2, concat_axis=1, tiled=True)]
    all_gather x1, blocking collectives: 39.4 us -> 18.3 us  [per_device(): lax.all_gather(w_out, 'ctx', axis=0, tiled=True)]
    ppermute x0 -> x7, waiting for transfers between devices: none -> 16.5 us  [_map_unit(): right_arr = lax.ppermute(right_arr, axis_name=bus_axis, perm=mid_arr)]
    all_gather x1 -> x0, blocking collectives: 11.5 us -> none  [per_device(): chains = lax.all_gather(chain_ids[0], 'ctx', axis=0, tiled=True)]
    all_gather x1, waiting for transfers between devices: 6.53 us -> 0.01 us  [per_device(): lax.all_gather(out_full_rows, 'expert', axis=1, tiled=True)]
    all_to_all x1, blocking collectives: 37.6 us -> 34 us  [per_device(): lax.all_to_all(outgoing, 'expert', split_axis=0, concat_axis=0, tiled=True)]
  transfers between devices with their start and end apart: 5 -> 12, of which waited for: 4 -> 10; matrix products, arithmetic and copies ran while one was open for 7% -> 11% of each run, Pallas kernels for 0% -> 0%
where the time goes in v1:
time: 266 us; the launch traced here: 265 us
  waiting for transfers between devices  101 us (38%)
  blocking collectives  76 us (29%)
  matrix products  24.9 us (9%)
  local copies, waits for them, and re-layouts  23.6 us (9%)
  starting transfers between devices  16.3 us (6%)
  between operations  13.7 us (5%)
  other arithmetic  9.72 us (4%)
    all_to_all x1, blocking collectives, per_device(): lax.all_to_all(outgoing, 'expert', split_axis=0, concat_axis=0, tiled=True)  34 us
    all_to_all x1, waiting for transfers between devices, per_device(): lax.all_to_all(projected, 'ctx', split_axis=2, concat_axis=1, tiled=True)  29.1 us
    all_to_all x1, waiting for transfers between devices, per_device(): lax.all_to_all(result.reshape(-1, count, width), 'expert', split_axis=0,...  27.5 us
    all_gather x1, blocking collectives, per_device(): lax.all_gather(w_qkv, 'ctx', axis=2, tiled=True)  23.7 us
    all_gather x1, blocking collectives, per_device(): lax.all_gather(w_out, 'ctx', axis=0, tiled=True)  18.3 us
    all_gather x1, waiting for transfers between devices, per_device(): lax.all_gather(qkv_columns, 'expert', axis=1, tiled=True)  17.4 us
    ppermute x7, waiting for transfers between devices, _map_unit(): right_arr = lax.ppermute(right_arr, axis_name=bus_axis, perm=mid_arr)  16.5 us
    all_to_all x1, waiting for transfers between devices, per_device(): lax.all_to_all(attended, 'ctx', split_axis=0, concat_axis=1, tiled=True)  10.1 us
  transfers between devices with their start and end apart: 12, of which 10 were waited for; matrix products, arithmetic and copies ran while one was open for 11% of the time, Pallas kernels for 0%

profile of v1, /device:TPU:1, one launch (start us, length us, event | category | flops | bytes accessed | tf_op | source)
XLA Modules:
  0.0 264.9 jit_solution(4581305023026038935)
XLA Ops:
  6.5 23.7 %all_gather.12 = bf16[3,32,1024]{2,1,0:T(8,128)(2,1)} all-gather(bf16[3,32,128]{2,1,0:T(8,128)(2,1)} %param.20), channel_id=1, replica_groups=mesh['ctx'=8,'expert'=32] {'ctx'}, dimensions={2}, use_global_device_ids=true | all-gather | bytes 221184 | tf_op jit(solution)/shard_map/all_gather | solution.py:82
  30.4 18.3 %all_gather.14 = bf16[1024,32]{0,1:T(8,128)(2,1)} all-gather(bf16[128,32]{0,1:T(8,128)(2,1)} %param.21), channel_id=1, replica_groups=mesh['ctx'=8,'expert'=32] {'ctx'}, dimensions={0}, use_global_device_ids=true | all-gather | bytes 73728 | tf_op jit(solution)/shard_map/all_gather | solution.py:83
  51.7 1.7 collective-permute-done.1
  53.4 1.7 reduce-window.6
  55.2 2.0 collective-permute-done.2
  57.5 3.3 %collective-permute-done.3 = s32[128]{0:T(128)S(1)} collective-permute-done((s32[128]{0:T(128)S(1)}, s32[128]{0:T(128)S(1)}, u32[]{:S(2)}, u32[]{:S(2)}) %collective-permute-start.3) | collective-permute-done | bytes 544 | tf_op jit(solution)/shard_map/ppermute | solution.py:15
  60.8 3.6 %collective-permute-done.4 = s32[128]{0:T(128)S(1)} collective-permute-done((s32[128]{0:T(128)S(1)}, s32[128]{0:T(128)S(1)}, u32[]{:S(2)}, u32[]{:S(2)}) %collective-permute-start.4) | collective-permute-done | bytes 544 | tf_op jit(solution)/shard_map/ppermute | solution.py:15
  64.6 3.4 %collective-permute-done.5 = s32[128]{0:T(128)S(1)} collective-permute-done((s32[128]{0:T(128)S(1)}, s32[128]{0:T(128)S(1)}, u32[]{:S(2)}, u32[]{:S(2)}) %collective-permute-start.5) | collective-permute-done | bytes 544 | tf_op jit(solution)/shard_map/ppermute | solution.py:15
  68.1 1.3 dynamic_slice.16
  69.3 2.3 collective-permute-done.6
  71.7 17.4 %all-gather.3.cloned.1.call-done = bf16[3,1024,1024]{2,1,0:T(8,128)(2,1)} async-done(((bf16[3,32,1024]{2,1,0:T(8,128)(2,1)}), bf16[3,1024,1024]{2,1,0:T(8,128)(2,1)}) %all-gather.3.cloned.1.call-update) | async-done | bytes 6291472 | tf_op jit(solution)/shard_map/all_gather | solution.py:88
  89.0 4.9 %fusion.21 = bf16[3,128,1024]{2,1,0:T(8,128)(2,1)} fusion(bf16[3,1024,1024]{2,1,0:T(8,128)(2,1)} %all-gather.3.cloned.1.call-done, bf16[1,128,1024]{2,1,0:T(8,128)(2,1)} %param.13, f32[1024]{0:T(1024)} %param.17, f32[128]{0:T(128)S(1)} %add_rsqrt_fusion.1), kind=kOutput, calls=%fused_computation.28 | convolution fusion | flops 806223872 | bytes 7344640 | tf_op jit(solution)/shard_map/tr,ird->itd/dot_general | solution.py:85
  93.9 2.4 copy.69
  96.3 6.7 %all-to-all-start = ((bf16[3,128,1024]{1,0,2:T(4,128)(2,1)}), bf16[3,128,1024]{1,0,2:T(4,128)(2,1)}, u32[]{:S(2)}, u32[]{:S(2)}) async-start(bf16[3,128,1024]{1,0,2:T(4,128)(2,1)} %copy.69), calls=%async_computation | async-start | bytes 2097152 | tf_op jit(solution)/shard_map/all_to_all | solution.py:91
  103.3 29.1 %all-to-all-done = bf16[3,128,1024]{1,0,2:T(4,128)(2,1)} async-done(((bf16[3,128,1024]{1,0,2:T(4,128)(2,1)}), bf16[3,128,1024]{1,0,2:T(4,128)(2,1)}, u32[]{:S(2)}, u32[]{:S(2)}) %all-to-all-start) | async-done | bytes 786464 | tf_op jit(solution)/shard_map/all_to_all | solution.py:91
  132.4 1.3 copy.70
  134.5 1.8 copy.71
  138.0 8.3 %while.10 = (s32[]{:T(128)}, bf16[2,512,1,128]{3,1,2,0:T(8,128)(2,1)}, bf16[2,512,1,128]{3,1,2,0:T(8,128)(2,1)}, bf16[1024,1,128]{2,0,1:T(8,128)(2,1)}, s32[2,51...) while((s32[]{:T(128)}, ...), condition=%wide.region_4.5_spmd, body=%wide.region_1.4_spmd.sunk | while | flops 273742848 | bytes 10245305 | solution.py:57
  138.0 2.3 fusion.58
  142.2 2.3 fusion.58
  146.3 3.6 %all-to-all-start.1 = ((bf16[8,128,128]{2,1,0:T(8,128)(2,1)}), bf16[8,128,128]{2,1,0:T(8,128)(2,1)S(1)}, u32[]{:S(2)}, u32[]{:S(2)}) async-start(bf16[8,128,128]{2,1,0:T(8,128)(2,1)} %bitcast.178), calls=%async_computation.1 | async-start | bytes 524288 | tf_op jit(solution)/shard_map/all_to_all | solution.py:93
  150.2 1.1 fusion.20
  151.4 10.1 %all-to-all-done.1 = bf16[8,128,128]{2,1,0:T(8,128)(2,1)S(1)} async-done(((bf16[8,128,128]{2,1,0:T(8,128)(2,1)}), bf16[8,128,128]{2,1,0:T(8,128)(2,1)S(1)}, u32[]{:S(2)}, u32[]{:S(2)}) %all-to-all-start.1) | async-done | bytes 262176 | tf_op jit(solution)/shard_map/all_to_all | solution.py:93
  162.3 2.6 multiply_reduce_fusion
  165.8 34.0 %all_to_all.44 = bf16[32,32,1024]{2,1,0:T(8,128)(2,1)S(1)} all-to-all(bf16[32,32,1024]{2,1,0:T(8,128)(2,1)S(1)} %bitcast.174), channel_id=1, replica_groups=mesh['ctx'=8,'expert'=32] {'expert'}, dimensions={0} | all-to-all | bytes 4194304 | tf_op jit(solution)/shard_map/all_to_all | solution.py:120
  199.8 6.1 %convolution_bitcast_fusion = f32[32,1,32,2816]{3,2,0,1:T(8,128)S(1)} fusion(bf16[32,32,1024]{2,1,0:T(8,128)(2,1)S(1)} %all_to_all.44, bf16[1,1024,2816]{2,1,0:T(8,128)(2,1)S(1)} %copy-done.8), kind=kOutput, calls=%fused_computation.14 | convolution fusion | flops 5905580032 | bytes 19398656 | tf_op jit(solution)/shard_map/sxcd,xdf->sxcf/dot_general | solution.py:123
  205.9 4.8 %fusion.15 = bf16[32,32,1024]{2,1,0:T(8,128)(2,1)} fusion(bf16[1,1408,1024]{2,1,0:T(8,128)(2,1)S(1)} %copy-done, f32[32,1,32,2816]{3,2,0,1:T(8,128)S(1)} %convolution_bitcast_fusion), kind=kOutput, calls=%fused_computation.23 | convolution fusion | flops 2962489344 | bytes 16515072 | tf_op jit(solution)/shard_map/sxcf,xfd->sxcd/dot_general | solution.py:125
  210.7 4.9 %all-to-all-start.3 = ((bf16[32,32,1024]{2,1,0:T(8,128)(2,1)}), bf16[32,32,1024]{2,1,0:T(8,128)(2,1)}, u32[]{:S(2)}, u32[]{:S(2)}) async-start(bf16[32,32,1024]{2,1,0:T(8,128)(2,1)} %fusion.15), calls=%async_computation.3 | async-start | bytes 4194304 | tf_op jit(solution)/shard_map/all_to_all | solution.py:128
  216.0 27.5 %all-to-all-done.3 = bf16[32,32,1024]{2,1,0:T(8,128)(2,1)} async-done(((bf16[32,32,1024]{2,1,0:T(8,128)(2,1)}), bf16[32,32,1024]{2,1,0:T(8,128)(2,1)}, u32[]{:S(2)}, u32[]{:S(2)}) %all-to-all-start.3) | async-done | bytes 2097184 | tf_op jit(solution)/shard_map/all_to_all | solution.py:128
  243.5 6.4 %gather_fusion = bf16[768,1024]{1,0:T(8,128)(2,1)} fusion(bf16[1024,1024]{1,0:T(8,128)(2,1)} %bitcast.38, s32[1024]{0:T(1024)S(1)} %pad_clamp_fusion), kind=kCustom, calls=%fused_computation | custom fusion | bytes 3148800 | tf_op jit(solution)/shard_map/jit(_take)/gather | solution.py:131
  249.9 3.7 %gather.7 = bf16[128,6,1024]{2,1,0:T(8,128)(2,1)} reshape(bf16[768,1024]{1,0:T(8,128)(2,1)} %gather_fusion) | data formatting | bytes 3145728 | tf_op jit(solution)/shard_map/jit(_take)/gather | solution.py:131
  253.5 3.4 %copy_select_fusion = bf16[128,6,1024]{2,0,1:T(8,128)(2,1)S(1)} fusion(bf16[128,6,1024]{2,1,0:T(8,128)(2,1)} %gather.7, pred[128,6]{0,1:T(8,128)(4,1)S(1)} %get-tuple-element.112), kind=kLoop, calls=%fused_computation.26 | loop fusion | flops 786432 | bytes 3146496 | tf_op jit(solution)/shard_map/jit(_take)/select_n | solution.py:131
  (91 shorter events, 13.2 us)
Async XLA Ops:
  6.5 199.4 %copy-start = (bf16[1,1408,1024]{2,1,0:T(8,128)(2,1)S(1)}, bf16[1,1408,1024]{2,1,0:T(8,128)(2,1)}, u32[]{:S(2)}) copy-start(bf16[1,1408,1024]{2,1,0:T(8,128)(2,1)} %param.23) | copy-start | bytes 8650756
  6.5 82.5 %all-gather.3.cloned.1.call-start = ((), (), s32[]{:S(2)}) async-start(), calls=%async_computation.4 | async-start | bytes 6488064 | tf_op jit(solution)/shard_map/all_gather | solution.py:88
  30.3 132.1 %all-gather.5.cloned.1.call-start = ((), (), s32[]{:S(2)}) async-start(), calls=%async_computation.5 | async-start | bytes 2162688 | tf_op jit(solution)/shard_map/all_gather | solution.py:96
  30.3 19.4 %collective-permute-start = (s32[128]{0:T(128)}, s32[128]{0:T(128)S(1)}, u32[]{:S(2)}, u32[]{:S(2)}) collective-permute-start(s32[128]{0:T(128)} %bitcast.185), channel_id=1, source_target_pairs={{0,32},{32,64},{64,96},{96,128},{128,160},{160,192},{192,224},{224... | collective-permute-start | bytes 1544 | tf_op jit(solution)/shard_map/ppermute | solution.py:15
  49.7 3.7 %collective-permute-start.1 = (s32[128]{0:T(128)S(1)}, s32[128]{0:T(128)S(1)}, u32[]{:S(2)}, u32[]{:S(2)}) collective-permute-start(s32[128]{0:T(128)S(1)} %collective-permute-done), channel_id=1, source_target_pairs={{0,32},{32,64},{64,96},{96,128},{128,160},{160,192},{192,224},{224... | collective-permute-start | bytes 1544 | tf_op jit(solution)/shard_map/ppermute | solution.py:15
  53.4 3.8 %collective-permute-start.2 = (s32[128]{0:T(128)S(1)}, s32[128]{0:T(128)S(1)}, u32[]{:S(2)}, u32[]{:S(2)}) collective-permute-start(s32[128]{0:T(128)S(1)} %collective-permute-done.1), channel_id=1, source_target_pairs={{0,32},{32,64},{64,96},{96,128},{128,160},{160,192},{192,224},{224... | collective-permute-start | bytes 1544 | tf_op jit(solution)/shard_map/ppermute | solution.py:15
  57.2 3.6 %collective-permute-start.3 = (s32[128]{0:T(128)S(1)}, s32[128]{0:T(128)S(1)}, u32[]{:S(2)}, u32[]{:S(2)}) collective-permute-start(s32[128]{0:T(128)S(1)} %collective-permute-done.2), channel_id=1, source_target_pairs={{0,32},{32,64},{64,96},{96,128},{128,160},{160,192},{192,224},{224... | collective-permute-start | bytes 1544 | tf_op jit(solution)/shard_map/ppermute | solution.py:15
  60.8 3.6 %collective-permute-start.4 = (s32[128]{0:T(128)S(1)}, s32[128]{0:T(128)S(1)}, u32[]{:S(2)}, u32[]{:S(2)}) collective-permute-start(s32[128]{0:T(128)S(1)} %collective-permute-done.3), channel_id=1, source_target_pairs={{0,32},{32,64},{64,96},{96,128},{128,160},{160,192},{192,224},{224... | collective-permute-start | bytes 1544 | tf_op jit(solution)/shard_map/ppermute | solution.py:15
  64.4 3.6 %collective-permute-start.5 = (s32[128]{0:T(128)S(1)}, s32[128]{0:T(128)S(1)}, u32[]{:S(2)}, u32[]{:S(2)}) collective-permute-start(s32[128]{0:T(128)S(1)} %collective-permute-done.4), channel_id=1, source_target_pairs={{0,32},{32,64},{64,96},{96,128},{128,160},{160,192},{192,224},{224... | collective-permute-start | bytes 1544 | tf_op jit(solution)/shard_map/ppermute | solution.py:15
  68.0 3.6 %collective-permute-start.6 = (s32[128]{0:T(128)S(1)}, s32[128]{0:T(128)S(1)}, u32[]{:S(2)}, u32[]{:S(2)}) collective-permute-start(s32[128]{0:T(128)S(1)} %collective-permute-done.5), channel_id=1, source_target_pairs={{0,32},{32,64},{64,96},{96,128},{128,160},{160,192},{192,224},{224... | collective-permute-start | bytes 1544 | tf_op jit(solution)/shard_map/ppermute | solution.py:15
  93.9 9.1 %copy-start.9 = (s32[1,128]{1,0:T(1,128)S(1)}, s32[1,128]{1,0:T(1,128)}, u32[]{:S(2)}) copy-start(s32[1,128]{1,0:T(1,128)} %param.14) | copy-start | bytes 1540
  96.3 36.1 %all-to-all-start = ((bf16[3,128,1024]{1,0,2:T(4,128)(2,1)}), bf16[3,128,1024]{1,0,2:T(4,128)(2,1)}, u32[]{:S(2)}, u32[]{:S(2)}) async-start(bf16[3,128,1024]{1,0,2:T(4,128)(2,1)} %copy.69), calls=%async_computation | async-start | bytes 2097152 | tf_op jit(solution)/shard_map/all_to_all | solution.py:91
  138.0 12.2 %copy-start.5 = (s32[1,128,6]{1,0,2:T(1,128)S(1)}, s32[1,128,6]{1,0,2:T(1,128)}, u32[]{:S(2)}) copy-start(s32[1,128,6]{1,0,2:T(1,128)} %param.15) | copy-start | bytes 9220
  138.0 2.8 %copy-start.2 = (bf16[2,512,1,128]{3,1,2,0:T(8,128)(2,1)S(1)}, bf16[2,512,1,128]{3,1,2,0:T(8,128)(2,1)}, u32[]{:S(2)}) copy-start(bf16[2,512,1,128]{3,1,2,0:T(8,128)(2,1)} %get-tuple-element.190) | copy-start | bytes 786436 | tf_op jit(solution)/shard_map/while
  138.0 2.8 %copy-start.4 = (bf16[1024,1,128]{2,0,1:T(8,128)(2,1)S(1)}, bf16[1024,1,128]{2,0,1:T(8,128)(2,1)}, u32[]{:S(2)}) copy-start(bf16[1024,1,128]{2,0,1:T(8,128)(2,1)} %get-tuple-element.205) | copy-start | bytes 786436 | tf_op jit(solution)/shard_map/while
  141.4 0.7 copy-start.3
  142.1 2.8 %copy-start.2 = (bf16[2,512,1,128]{3,1,2,0:T(8,128)(2,1)S(1)}, bf16[2,512,1,128]{3,1,2,0:T(8,128)(2,1)}, u32[]{:S(2)}) copy-start(bf16[2,512,1,128]{3,1,2,0:T(8,128)(2,1)} %get-tuple-element.190) | copy-start | bytes 786436 | tf_op jit(solution)/shard_map/while
  142.1 2.8 %copy-start.4 = (bf16[1024,1,128]{2,0,1:T(8,128)(2,1)S(1)}, bf16[1024,1,128]{2,0,1:T(8,128)(2,1)}, u32[]{:S(2)}) copy-start(bf16[1024,1,128]{2,0,1:T(8,128)(2,1)} %get-tuple-element.205) | copy-start | bytes 786436 | tf_op jit(solution)/shard_map/while
  145.6 0.7 copy-start.3
  146.3 15.2 %all-to-all-start.1 = ((bf16[8,128,128]{2,1,0:T(8,128)(2,1)}), bf16[8,128,128]{2,1,0:T(8,128)(2,1)S(1)}, u32[]{:S(2)}, u32[]{:S(2)}) async-start(bf16[8,128,128]{2,1,0:T(8,128)(2,1)} %bitcast.178), calls=%async_computation.1 | async-start | bytes 524288 | tf_op jit(solution)/shard_map/all_to_all | solution.py:93
  149.9 15.1 %copy-start.6 = (f32[1024]{0:T(1024)S(1)}, f32[1024]{0:T(1024)}, u32[]{:S(2)}) copy-start(f32[1024]{0:T(1024)} %param.18) | copy-start | bytes 12292
  162.3 2.6 copy-start.1
  165.0 34.8 %copy-start.8 = (bf16[1,1024,2816]{2,1,0:T(8,128)(2,1)S(1)}, bf16[1,1024,2816]{2,1,0:T(8,128)(2,1)}, u32[]{:S(2)}) copy-start(bf16[1,1024,2816]{2,1,0:T(8,128)(2,1)} %param.22) | copy-start | bytes 17301508
  210.7 5.2 %copy-start.7 = (f32[1,128,6]{1,0,2:T(1,128)S(1)}, f32[1,128,6]{1,0,2:T(1,128)}, u32[]{:S(2)}) copy-start(f32[1,128,6]{1,0,2:T(1,128)} %param.16) | copy-start | bytes 9220
  210.7 32.7 %all-to-all-start.3 = ((bf16[32,32,1024]{2,1,0:T(8,128)(2,1)}), bf16[32,32,1024]{2,1,0:T(8,128)(2,1)}, u32[]{:S(2)}, u32[]{:S(2)}) async-start(bf16[32,32,1024]{2,1,0:T(8,128)(2,1)} %fusion.15), calls=%async_computation.3 | async-start | bytes 4194304 | tf_op jit(solution)/shard_map/all_to_all | solution.py:128
Sparse Core Ops, SparseCore 0:
  30.4 58.6 all-gather.2
  91.6 47.7 all-gather.4
